TPU v7x, 32 devices: a whole 2x2x4 slice. The times are simulated.
32 devices in a mesh: pipe: 2 (over core), seq: 16 (over z, y, x).
Axes of the slice: x: 2, y: 2, z: 4, core: 2. Of those that a mesh axis runs over, the one named last changes fastest.
Arguments:
- queries: bfloat16 [2, 1024, 4096], P('pipe', 'seq'), may hold values from -6 to 6
- keys: bfloat16 [2, 1024, 4096], P('pipe', 'seq'), may hold values from -6 to 6
- values: bfloat16 [2, 1024, 4096], P('pipe', 'seq'), may hold values from -6 to 6
- out_weight: bfloat16 [2, 4096, 5120], P('pipe', None, 'seq'), may hold values from -0.375 to 0.375
- head_class: int32 [2, 32], P('pipe'), may hold values from 0 to 1
- kv_blocks: int32 [2, 32, 16, 16], P('pipe'), may hold values from 0 to 15, as said below
- kv_count: int32 [2, 32], P('pipe'), may hold values from 1 to 16, as said below
Outputs:
- handed: bfloat16 [2, 1024, 5120], P('pipe', 'seq')
Inputs may be any that keep to these rules, and one draw needn't show every extreme that they name: `kv_blocks`: in every row the entries are distinct, and the first is the query block itself. `kv_count`: in every section some head uses all 16 entries.
All inputs are finite; a program needn't handle non-finite values.
Results may differ from a plain program's by a relative error of at most 0.018.
Values may be sent and summed in bfloat16 or wider, within the bound.
A program may use at most 64 MiB of HBM per device.

v0:
```python
import jax
import jax.numpy as jnp
from jax import lax
from jax.sharding import PartitionSpec as P

FRAMES = 4
BLOCK = 64


def from_behind(value, axis, steps):
    count = lax.axis_size(axis)
    pairs = [(source, (source + steps) % count) for source in range(count)]
    return lax.ppermute(value, axis, pairs)


def frame_to_pos(tensor):
    token_total, row_width = tensor.shape
    return (
        tensor.reshape(FRAMES, token_total // FRAMES, row_width)
        .transpose(1, 0, 2)
        .reshape(token_total, row_width)
    )


def pos_to_frame(tensor):
    token_total, row_width = tensor.shape
    return (
        tensor.reshape(token_total // FRAMES, FRAMES, row_width)
        .transpose(1, 0, 2)
        .reshape(token_total, row_width)
    )


def attend_head(query_rows, key_rows, value_rows, temporal, blocks, live_count):
    token_total, head_width = query_rows.shape
    nblock = token_total // BLOCK
    query_rows, key_rows, value_rows = lax.cond(
        temporal,
        lambda tensors: tuple((frame_to_pos(tensor) for tensor in tensors)),
        lambda tensors: tensors,
        (query_rows, key_rows, value_rows),
    )
    query_tiles = query_rows.reshape(nblock, BLOCK, head_width)
    key_blocks = key_rows.reshape(nblock, BLOCK, head_width)
    value_blocks = value_rows.reshape(nblock, BLOCK, head_width)
    score_scale = head_width ** (-0.5)
    columns = jnp.arange(2 * BLOCK)

    def advance(pair_index, state_now):
        running_max, weight_sum, numerator = state_now
        chosen = lax.dynamic_slice_in_dim(blocks, 2 * pair_index, 2, 1)
        selected_keys = key_blocks[chosen].reshape(nblock, 2 * BLOCK, head_width)
        selected_values = value_blocks[chosen].reshape(nblock, 2 * BLOCK, head_width)
        logit_scores = (
            jnp.einsum(
                "ure,ute->urt", query_tiles, selected_keys, preferred_element_type=jnp.float32
            )
            * score_scale
        )
        usable = (columns < BLOCK) | (2 * pair_index + 1 < live_count)
        logit_scores = jnp.where(usable[None, None, :], logit_scores, -jnp.inf)
        newest_max = jnp.maximum(running_max, jnp.max(logit_scores, axis=-1))
        weights_now = jnp.exp(logit_scores - newest_max[..., None])
        factor = jnp.exp(running_max - newest_max)
        weight_sum = weight_sum * factor + jnp.sum(weights_now, axis=-1)
        numerator = numerator * factor[..., None] + jnp.einsum(
            "yhn,yng->yhg",
            weights_now.astype(jnp.bfloat16),
            selected_values,
            preferred_element_type=jnp.float32,
        )
        return (newest_max, weight_sum, numerator)

    initial = (
        jnp.full((nblock, BLOCK), -jnp.inf, jnp.float32),
        jnp.zeros((nblock, BLOCK), jnp.float32),
        jnp.zeros((nblock, BLOCK, head_width), jnp.float32),
    )
    running_max, weight_sum, numerator = lax.fori_loop(0, (live_count + 1) // 2, advance, initial)
    result = (numerator / weight_sum[..., None]).reshape(token_total, head_width)
    result = lax.cond(temporal, pos_to_frame, lambda tensor: tensor, result)
    return result.astype(jnp.bfloat16)


def shards(queries, keys, values, out_weight, head_class, kv_blocks, kv_count):
    members = lax.axis_size("seq")
    head_total = head_class.shape[1]
    per_dev = head_total // members
    head_width = queries.shape[2] // head_total
    classes = head_class[0]
    blocks = kv_blocks[0]
    counts = kv_count[0]
    query_rows = queries[0]
    key_rows = keys[0]
    value_rows = values[0]
    weight_local = out_weight[0]
    placing = jnp.arange(head_total, dtype=jnp.int32)
    exchanged = (
        lax.all_to_all(query_rows, "seq", split_axis=1, concat_axis=0, tiled=True),
        lax.all_to_all(key_rows, "seq", split_axis=1, concat_axis=0, tiled=True),
        lax.all_to_all(value_rows, "seq", split_axis=1, concat_axis=0, tiled=True),
    )
    own_heads = lax.dynamic_slice_in_dim(placing, lax.axis_index("seq") * per_dev, per_dev)
    results = []
    for slot in range(per_dev):
        head_now = own_heads[slot]
        lo_col = slot * head_width
        hi_col = lo_col + head_width
        results.append(
            attend_head(
                exchanged[0][:, lo_col:hi_col],
                exchanged[1][:, lo_col:hi_col],
                exchanged[2][:, lo_col:hi_col],
                classes[head_now] == 1,
                blocks[head_now],
                counts[head_now],
            )
        )
    joined = jnp.concatenate(results, axis=1)
    weight_mine = lax.all_to_all(weight_local, "seq", split_axis=0, concat_axis=1, tiled=True)
    projected = lax.psum_scatter(
        jnp.dot(joined, weight_mine, preferred_element_type=jnp.float32).astype(jnp.bfloat16),
        "seq",
        scatter_dimension=0,
        tiled=True,
    )
    handed = from_behind(projected, "pipe", 1)
    return handed[None]


def solution(mesh):
    placed = (
        P("pipe", "seq", None),
        P("pipe", "seq", None),
        P("pipe", "seq", None),
        P("pipe", None, "seq"),
        P("pipe", None),
        P("pipe", None, None, None),
        P("pipe", None),
    )
    return jax.shard_map(
        shards, mesh=mesh, in_specs=placed, out_specs=P("pipe", "seq", None), check_vma=False
    )
```

profile of v0, /device:TPU:9, one launch (start us, length us, event | category | flops | bytes accessed | tf_op | source)
XLA Modules:
  0.0 367.4 jit_solution(3479993437951516926)
XLA Ops:
  6.5 1.2 copy.62
  7.7 0.0 copy-start.1
  7.8 1.0 copy.55
  8.7 6.7 %all-to-all-start = ((bf16[64,16,256]{2,0,1:T(8,128)(2,1)}), bf16[64,16,256]{2,0,1:T(8,128)(2,1)S(1)}, u32[]{:S(2)}, u32[]{:S(2)}) async-start(bf16[64,16,256]{2,0,1:T(8,128)(2,1)} %copy.55), calls=%async_computation | async-start | bytes 1048576 | tf_op jit(solution)/shard_map/all_to_all | solution.py:99
  15.4 0.1 copy.63
  15.5 0.0 copy-start.4
  15.5 0.0 copy-start.2
  15.5 1.0 copy.56
  16.5 12.2 %all-to-all-done = bf16[64,16,256]{2,0,1:T(8,128)(2,1)S(1)} async-done(((bf16[64,16,256]{2,0,1:T(8,128)(2,1)}), bf16[64,16,256]{2,0,1:T(8,128)(2,1)S(1)}, u32[]{:S(2)}, u32[]{:S(2)}) %all-to-all-start) | async-done | bytes 524320 | tf_op jit(solution)/shard_map/all_to_all | solution.py:99
  28.6 5.0 %all-to-all-start.1 = ((bf16[64,16,256]{2,0,1:T(8,128)(2,1)}), bf16[64,16,256]{2,0,1:T(8,128)(2,1)S(1)}, u32[]{:S(2)}, u32[]{:S(2)}) async-start(bf16[64,16,256]{2,0,1:T(8,128)(2,1)} %copy.56), calls=%async_computation.1 | async-start | bytes 1048576 | tf_op jit(solution)/shard_map/all_to_all | solution.py:100
  33.7 0.1 copy.64
  33.8 1.0 copy.57
  34.7 12.1 %all-to-all-done.1 = bf16[64,16,256]{2,0,1:T(8,128)(2,1)S(1)} async-done(((bf16[64,16,256]{2,0,1:T(8,128)(2,1)}), bf16[64,16,256]{2,0,1:T(8,128)(2,1)S(1)}, u32[]{:S(2)}, u32[]{:S(2)}) %all-to-all-start.1) | async-done | bytes 524320 | tf_op jit(solution)/shard_map/all_to_all | solution.py:100
  46.8 5.0 %all-to-all-start.2 = ((bf16[64,16,256]{2,0,1:T(8,128)(2,1)}), bf16[64,16,256]{2,0,1:T(8,128)(2,1)S(1)}, u32[]{:S(2)}, u32[]{:S(2)}) async-start(bf16[64,16,256]{2,0,1:T(8,128)(2,1)} %copy.57), calls=%async_computation.2 | async-start | bytes 1048576 | tf_op jit(solution)/shard_map/all_to_all | solution.py:101
  51.8 0.1 dynamic_slice.27
  51.9 0.6 fusion.22
  56.0 0.6 constant_dynamic-slice_fusion.4
  59.1 0.1 constant_dynamic-slice_fusion.3
  59.3 0.1 copy.60
  59.4 0.2 copy.61
  59.6 2.6 copy.65
  62.2 2.5 copy.59
  64.7 0.2 all-to-all-done.2
  64.9 6.1 %all-to-all-start.3 = ((bf16[16,256,320]{1,2,0:T(8,128)(2,1)}), bf16[16,256,320]{1,2,0:T(8,128)(2,1)}, u32[]{:S(2)}, u32[]{:S(2)}) async-start(bf16[16,256,320]{1,2,0:T(8,128)(2,1)} %copy.59), calls=%async_computation.3 | async-start | bytes 5242880 | tf_op jit(solution)/shard_map/all_to_all | solution.py:120
  71.0 0.0 reduce-scatter.2.cloned.1.call-start
  71.1 0.7 conditional.12
  71.1 0.2 copy.50
  71.4 0.2 copy.51
  71.6 0.2 copy.52
  71.8 0.1 conditional.10
  72.0 7.2 %while.31 = (s32[]{:T(128)}, f32[16,64]{1,0:T(8,128)S(1)}, f32[16,64]{1,0:T(8,128)S(1)}, f32[16,64,128]{2,1,0:T(8,128)S(1)}, s32[]{:T(128)}, /*index=5*/s32[]{:T...) while((s32[]{:T(128)}, f32[16,64]{1,0:T(8,128)S(1)}, ...), condition=%wide.region_13.14_spmd.clone, body=%wide.region_10.13_spmd.clone.sunk | while | flops 68291944 | bytes 6100301 | solution.py:79
  72.7 0.1 compare_select_fusion.5
  72.7 0.1 reshape.231
  72.8 0.6 gather_fusion.3
  73.5 0.6 gather_fusion.2
  74.1 0.5 fusion.52
  74.7 0.4 fusion.53
  75.1 0.4 convolution_add_fusion.5
  76.2 0.1 compare_select_fusion.5
  76.3 0.1 reshape.231
  76.4 0.6 gather_fusion.3
  77.1 0.6 gather_fusion.2
  77.7 0.5 fusion.52
  78.3 0.4 fusion.53
  78.7 0.4 convolution_add_fusion.5
  79.2 0.2 broadcast_divide_fusion
  79.4 0.2 conditional.13
  79.4 0.1 copy.112
  79.6 3.5 while.30
  80.2 0.1 compare_select_fusion.4
  80.3 0.1 reshape.226
  80.4 0.6 gather_fusion.1
  81.0 0.6 gather_fusion
  81.7 0.5 fusion.46
  82.3 0.4 fusion.47
  82.7 0.4 convolution_add_fusion.4
  83.1 0.2 broadcast_divide_fusion.1
  83.4 44.3 %all-to-all-done.3 = bf16[16,256,320]{1,2,0:T(8,128)(2,1)} async-done(((bf16[16,256,320]{1,2,0:T(8,128)(2,1)}), bf16[16,256,320]{1,2,0:T(8,128)(2,1)}, u32[]{:S(2)}, u32[]{:S(2)}) %all-to-all-start.3) | async-done | bytes 2621472 | tf_op jit(solution)/shard_map/all_to_all | solution.py:120
  127.7 7.3 %convolution_convert_fusion = bf16[1024,5120]{1,0:T(8,128)(2,1)} fusion(bf16[256,5120]{0,1:T(8,128)(2,1)} %bitcast.47, bf16[1024,128]{1,0:T(8,128)(2,1)S(1)} %get-tuple-element.566, bf16[1024,128]{1,0:T(8,128)(2,1)S(1)} %get-tuple-element.565), kind=kOutput, calls=%fused_computation.32 | convolution fusion | flops 2690646016 | bytes 13631488 | tf_op jit(solution)/shard_map/dot_general | solution.py:122
  135.0 0.0 reduce-scatter.2.cloned.1.call-update
  135.0 221.1 %reduce-scatter.2.cloned.1.call-done = bf16[64,5120]{1,0:T(8,128)(2,1)} async-done(((bf16[1024,5120]{1,0:T(8,128)(2,1)}), bf16[64,5120]{1,0:T(8,128)(2,1)}) %reduce-scatter.2.cloned.1.call-update) | async-done | bytes 655376 | tf_op jit(solution)/shard_map/reduce_scatter | solution.py:121
  356.1 1.7 collective-permute-start
  357.8 1.9 collective-permute-done
  359.7 0.8 copy.113
  (37 shorter events, 0.4 us)
Async XLA Ops:
  6.5 8.8 %copy-start = (bf16[1,64,4096]{2,1,0:T(8,128)(2,1)S(1)}, bf16[1,64,4096]{2,1,0:T(8,128)(2,1)}, u32[]{:S(2)}) copy-start(bf16[1,64,4096]{2,1,0:T(8,128)(2,1)} %param.20) | copy-start | bytes 1572868
  7.7 25.9 %copy-start.1 = (bf16[1,64,4096]{2,1,0:T(8,128)(2,1)S(1)}, bf16[1,64,4096]{2,1,0:T(8,128)(2,1)}, u32[]{:S(2)}) copy-start(bf16[1,64,4096]{2,1,0:T(8,128)(2,1)} %param.21) | copy-start | bytes 1572868
  8.7 19.9 %all-to-all-start = ((bf16[64,16,256]{2,0,1:T(8,128)(2,1)}), bf16[64,16,256]{2,0,1:T(8,128)(2,1)S(1)}, u32[]{:S(2)}, u32[]{:S(2)}) async-start(bf16[64,16,256]{2,0,1:T(8,128)(2,1)} %copy.55), calls=%async_computation | async-start | bytes 1048576 | tf_op jit(solution)/shard_map/all_to_all | solution.py:99
  15.5 40.5 %copy-start.3 = (s32[1,32]{1,0:T(1,128)S(1)}, s32[1,32]{1,0:T(1,128)}, u32[]{:S(2)}) copy-start(s32[1,32]{1,0:T(1,128)} %param.25) | copy-start | bytes 388
  15.5 40.5 %copy-start.4 = (s32[1,32]{1,0:T(1,128)S(1)}, s32[1,32]{1,0:T(1,128)}, u32[]{:S(2)}) copy-start(s32[1,32]{1,0:T(1,128)} %param.23) | copy-start | bytes 388
  15.5 43.6 %copy-start.2 = (s32[1,32,16,16]{1,3,2,0:T(8,128)S(1)}, s32[1,32,16,16]{1,3,2,0:T(8,128)}, u32[]{:S(2)}) copy-start(s32[1,32,16,16]{1,3,2,0:T(8,128)} %param.24) | copy-start | bytes 98308
  28.6 18.2 %all-to-all-start.1 = ((bf16[64,16,256]{2,0,1:T(8,128)(2,1)}), bf16[64,16,256]{2,0,1:T(8,128)(2,1)S(1)}, u32[]{:S(2)}, u32[]{:S(2)}) async-start(bf16[64,16,256]{2,0,1:T(8,128)(2,1)} %copy.56), calls=%async_computation.1 | async-start | bytes 1048576 | tf_op jit(solution)/shard_map/all_to_all | solution.py:100
  46.8 18.1 %all-to-all-start.2 = ((bf16[64,16,256]{2,0,1:T(8,128)(2,1)}), bf16[64,16,256]{2,0,1:T(8,128)(2,1)S(1)}, u32[]{:S(2)}, u32[]{:S(2)}) async-start(bf16[64,16,256]{2,0,1:T(8,128)(2,1)} %copy.57), calls=%async_computation.2 | async-start | bytes 1048576 | tf_op jit(solution)/shard_map/all_to_all | solution.py:101
  64.9 62.8 %all-to-all-start.3 = ((bf16[16,256,320]{1,2,0:T(8,128)(2,1)}), bf16[16,256,320]{1,2,0:T(8,128)(2,1)}, u32[]{:S(2)}, u32[]{:S(2)}) async-start(bf16[16,256,320]{1,2,0:T(8,128)(2,1)} %copy.59), calls=%async_computation.3 | async-start | bytes 5242880 | tf_op jit(solution)/shard_map/all_to_all | solution.py:120
  71.0 285.1 %reduce-scatter.2.cloned.1.call-start = ((), (), s32[]{:S(2)}) async-start(), calls=%async_computation.5 | async-start | bytes 11141120 | tf_op jit(solution)/shard_map/reduce_scatter | solution.py:121
  356.1 3.6 collective-permute-start
Sparse Core Ops, SparseCore 0:
  135.1 220.9 reduce-scatter.1
where the time goes:
time: 372 us; the launch traced here: 367 us
  waiting for transfers between devices  292 us (78%)
  starting transfers between devices  24.5 us (7%)
  between operations  19.6 us (5%)
  local copies, waits for them, and re-layouts  17 us (5%)
  matrix products  10.2 us (3%)
    reduce_scatter x1, waiting for transfers between devices, shards(): lax.psum_scatter(jnp.dot(joined, weight_mine, preferred_element_type=jnp....  221 us
    all_to_all x1, waiting for transfers between devices, shards(): lax.all_to_all(weight_local, 'seq', split_axis=0, concat_axis=1, tiled=True)  44.3 us
    all_to_all x1, waiting for transfers between devices, shards(): lax.all_to_all(query_rows, 'seq', split_axis=1, concat_axis=0, tiled=True)  12.2 us
    all_to_all x1, waiting for transfers between devices, shards(): lax.all_to_all(key_rows, 'seq', split_axis=1, concat_axis=0, tiled=True)  12.1 us
  transfers between devices with their start and end apart: 6, of which 6 were waited for; matrix products, arithmetic and copies ran while one was open for 5% of the time, Pallas kernels for 0%

commit v1 on v0

v1 whole, which is shorter than its diff:
```python
import functools

import jax
import jax.numpy as jnp
from jax import lax
from jax.experimental import pallas as pl
from jax.experimental.pallas import tpu as pltpu
from jax.sharding import PartitionSpec as P

FRAMES = 4
BLOCK = 64
MASKED = 131072.0
LOG2E = 1.4426950408889634
MESH = pl.DeviceIdType.MESH


def kernel(
    members, per_dev, stages,
    classes, counts, lists, queries, keys, values, weight,
    out,
    qbuf, kbuf, vbuf, ebuf, bbuf, abuf, wown, wpart, cown, cpart, csend, crecv, osend, obuf,
    qkv_send, qkv_recv, qkv_local, w_sems, w_local, a_send, f_send, a_recv, c_send, c_recv,
    o_send, o_recv,
):
    stage = lax.axis_index("pipe")
    me = lax.axis_index("seq")
    half = lax.rem(me, 2)
    col = me // 2
    side = lax.rem(col, 2)
    level = col // 2
    levels = members // 4
    partner = me + 1 - 2 * half
    across_col = col + 1 - 2 * side
    across = 2 * across_col + half
    following = lax.rem(stage + 1, stages)
    preceding = lax.rem(stage + stages - 1, stages)
    rows, width = queries.shape[0], kbuf.shape[-1]
    tokens = rows * members
    tensors = ((queries, qbuf), (keys, kbuf), (values, vbuf))

    def level_col(r):
        return lax.rem(level + r, levels) * 2

    barrier = pltpu.get_barrier_semaphore()

    def greet(r, carry):
        pl.semaphore_signal(
            barrier, inc=1, device_id={"seq": lax.rem(me + r, members)}, device_id_type=MESH
        )
        return carry

    def greet_preceding(r, carry):
        pl.semaphore_signal(barrier, inc=1, device_id=(preceding, r), device_id_type=MESH)
        return carry

    lax.fori_loop(1, members, greet, 0)
    lax.fori_loop(0, members, greet_preceding, 0)
    weight_copy = pltpu.make_async_copy(weight.at[:, half], wown, w_local)
    weight_copy.start()

    def head_columns(owner, slot):
        return pl.ds(pl.multiple_of((owner * per_dev + slot) * width, width), width)

    mine = pl.ds(pl.multiple_of(me * rows, rows), rows)
    own_copies = []
    for slot in range(per_dev):
        for which, (source, landing) in enumerate(tensors):
            copy = pltpu.make_async_copy(
                source.at[:, head_columns(me, slot)],
                landing.at[slot, mine],
                qkv_local.at[slot, which],
            )
            copy.start()
            own_copies.append(copy)
    pl.semaphore_wait(barrier, 2 * members - 1)

    for slot in range(per_dev):

        def send(r, carry):
            peer = lax.rem(me + r, members)
            for which, (source, landing) in enumerate(tensors):
                pltpu.make_async_remote_copy(
                    src_ref=source.at[:, head_columns(peer, slot)],
                    dst_ref=landing.at[slot, mine],
                    send_sem=qkv_send.at[slot, which],
                    recv_sem=qkv_recv.at[slot, which],
                    device_id={"seq": peer},
                    device_id_type=MESH,
                ).start()
            return carry

        lax.fori_loop(1, members, send, 0)
    weight_swap = pltpu.make_async_remote_copy(
        src_ref=weight.at[:, 1 - half],
        dst_ref=wpart,
        send_sem=w_sems.at[0],
        recv_sem=w_sems.at[1],
        device_id={"seq": partner},
        device_id_type=MESH,
    )
    weight_swap.start()

    nblock = lists.shape[1]
    token = lax.broadcasted_iota(jnp.int32, (tokens, width), 0)
    lane = lax.broadcasted_iota(jnp.int32, (tokens, width), 1)
    spatial = token // BLOCK
    temporal = lax.rem(token, tokens // FRAMES) // (BLOCK // FRAMES)
    listed_lane = lax.broadcasted_iota(jnp.int32, (nblock, width), 1)
    for slot in range(per_dev):
        head = me * per_dev + slot
        block_of = jnp.where(classes[0, head] == 1, temporal, spatial)
        member = jnp.where(block_of == lane, 1.0, 0.0).astype(jnp.bfloat16)
        ebuf[slot] = member
        entries = lists[head]
        offset = jnp.full((nblock, width), -MASKED, jnp.float32)
        for entry in range(entries.shape[1]):
            level_here = jnp.where(entry < counts[0, head], 0.0, -MASKED)
            offset = jnp.maximum(
                offset, jnp.where(entries[:, entry : entry + 1] == listed_lane, level_here, -MASKED)
            )
        offset = jnp.concatenate(
            [offset, jnp.zeros((width - nblock, width), jnp.float32)], axis=0
        ).astype(jnp.bfloat16)
        bbuf[slot] = lax.dot_general(
            member, offset, (((1,), (1,)), ((), ())), preferred_element_type=jnp.float32
        ).astype(jnp.bfloat16)
    cown[...] = jnp.zeros_like(cown)
    cpart[...] = jnp.zeros_like(cpart)
    for copy in own_copies:
        copy.wait()

    tile = 256
    scale = LOG2E * width ** (-0.5)
    others = pl.ds(0, tokens - rows)

    def shard_copy(source_col, slot, target, send_sem):
        return pltpu.make_async_remote_copy(
            src_ref=abuf.at[source_col, slot],
            dst_ref=abuf.at[source_col, slot],
            send_sem=send_sem,
            recv_sem=a_recv.at[source_col, slot],
            device_id={"seq": target},
            device_id_type=MESH,
        )

    def received(source_col, slot):
        pltpu.make_async_copy(
            abuf.at[source_col, slot], abuf.at[source_col, slot], a_recv.at[source_col, slot]
        ).wait()

    for slot in range(per_dev):
        for which, (source, landing) in enumerate(tensors):
            span = landing.at[slot, others]
            pltpu.make_async_copy(span, span, qkv_recv.at[slot, which]).wait()

        def attend(step, carry):
            here = pl.ds(pl.multiple_of(step * tile, tile), tile)
            wide_query = jnp.concatenate([qbuf[slot, here], ebuf[slot, here]], axis=1)
            wide_key = jnp.concatenate([kbuf[slot], bbuf[slot]], axis=1)
            scores = lax.dot_general(
                wide_query, wide_key, (((1,), (1,)), ((), ())), preferred_element_type=jnp.float32
            )
            top = jnp.max(scores, axis=1, keepdims=True)
            probs = jnp.exp2((scores - top) * scale).astype(jnp.bfloat16)
            wide_value = jnp.concatenate(
                [vbuf[slot], jnp.ones((tokens, width), jnp.bfloat16)], axis=1
            )
            sums = jnp.dot(probs, wide_value, preferred_element_type=jnp.float32)
            abuf[col, slot, here] = (sums[:, :width] / sums[:, width:]).astype(jnp.bfloat16)
            return carry

        lax.fori_loop(0, tokens // tile, attend, 0)
        shard_copy(col, slot, across, a_send.at[slot, 0]).start()

        def spread(r, carry):
            shard_copy(col, slot, 2 * (level_col(r) + side) + half, a_send.at[slot, r]).start()
            return carry

        lax.fori_loop(1, levels, spread, 0)

    weight_copy.wait()
    weight_swap.wait_recv()

    def shares(source_col, here):
        piece = jnp.concatenate([abuf[source_col, s, here] for s in range(per_dev)], axis=1)
        return (
            jnp.dot(piece, wown[source_col], preferred_element_type=jnp.float32),
            jnp.dot(piece, wpart[source_col], preferred_element_type=jnp.float32),
        )

    def accumulate(source_col):
        def part(step, carry):
            here = pl.ds(pl.multiple_of(step * tile, tile), tile)
            to_own, to_part = shares(source_col, here)
            cown[here] += to_own
            cpart[here] += to_part
            return carry

        lax.fori_loop(0, tokens // tile, part, 0)

    accumulate(col)

    def pass_on(r, carry):
        source_col = level_col(r) + side
        for slot in range(per_dev):
            received(source_col, slot)
            shard_copy(source_col, slot, across, f_send.at[slot, r]).start()
        accumulate(source_col)
        return carry

    lax.fori_loop(1, levels, pass_on, 0)

    def take_in(r, carry):
        source_col = level_col(r) + 1 - side
        for slot in range(per_dev):
            received(source_col, slot)
        accumulate(source_col)
        return carry

    lax.fori_loop(0, levels - 1, take_in, 0)
    last_col = level_col(levels - 1) + 1 - side
    for slot in range(per_dev):
        received(last_col, slot)

    chunks = tokens // tile

    def chunk_copy(here, chunk):
        return pltpu.make_async_remote_copy(
            src_ref=csend.at[here],
            dst_ref=crecv.at[here],
            send_sem=c_send.at[chunk],
            recv_sem=c_recv.at[chunk],
            device_id={"seq": partner},
            device_id_type=MESH,
        )

    def chunk_rows(chunk):
        return pl.ds(pl.multiple_of(chunk * tile, tile), tile)

    def finish(step, carry):
        chunk = lax.rem(step + col, chunks)
        here = chunk_rows(chunk)
        to_own, to_part = shares(last_col, here)
        csend[here] = (cpart[here] + to_part).astype(jnp.bfloat16)
        chunk_copy(here, chunk).start()
        cown[here] += to_own
        return carry

    lax.fori_loop(0, chunks, finish, 0)

    def row_copy(owner):
        return pltpu.make_async_remote_copy(
            src_ref=osend.at[pl.ds(pl.multiple_of(owner * rows, rows), rows)],
            dst_ref=obuf.at[me],
            send_sem=o_send.at[owner],
            recv_sem=o_recv.at[me],
            device_id=(following, owner),
            device_id_type=MESH,
        )

    def hand(step, carry):
        chunk = lax.rem(step + col, chunks)
        here = chunk_rows(chunk)
        chunk_copy(here, chunk).wait_recv()
        osend[here] = (cown[here] + crecv[here].astype(jnp.float32)).astype(jnp.bfloat16)
        for owner in range(tile // rows):
            row_copy(chunk * (tile // rows) + owner).start()
        return carry

    lax.fori_loop(0, chunks, hand, 0)

    for slot in range(per_dev):
        for which, (source, landing) in enumerate(tensors):
            span = landing.at[slot, others]
            pltpu.make_async_copy(span, span, qkv_send.at[slot, which]).wait()
        shard_copy(col, slot, across, a_send.at[slot, 0]).wait_send()

        def left(r, carry):
            shard_copy(col, slot, across, a_send.at[slot, r]).wait_send()
            shard_copy(level_col(r) + side, slot, across, f_send.at[slot, r]).wait_send()
            return carry

        lax.fori_loop(1, levels, left, 0)
    weight_swap.wait_send()

    def chunk_left(chunk, carry):
        chunk_copy(chunk_rows(chunk), chunk).wait_send()
        return carry

    lax.fori_loop(0, chunks, chunk_left, 0)

    def arrived(source, carry):
        row_copy(source).wait_send()
        pltpu.make_async_copy(obuf.at[source], obuf.at[source], o_recv.at[source]).wait()
        return carry

    lax.fori_loop(0, members, arrived, 0)
    pair = 2 * obuf.shape[2]
    for i in range(members // 2):
        out[:, i * pair : (i + 1) * pair] = jnp.concatenate([obuf[2 * i], obuf[2 * i + 1]], axis=1)


def shards(stages, queries, keys, values, out_weight, head_class, kv_blocks, kv_count):
    members = lax.axis_size("seq")
    heads = head_class.shape[1]
    per_dev = heads // members
    rows, total = queries.shape[1:]
    width = total // heads
    tokens = rows * members
    out_cols = out_weight.shape[2]
    cols = members // 2
    depth = per_dev * width
    weight = out_weight[0].reshape(cols, 2, depth, out_cols)
    bf16, f32 = jnp.bfloat16, jnp.float32
    dma = pltpu.SemaphoreType.DMA
    vmem = pl.BlockSpec(memory_space=pltpu.VMEM)
    smem = pl.BlockSpec(memory_space=pltpu.SMEM)
    head_buffer = pltpu.VMEM((per_dev, tokens, width), bf16)
    levels = members // 4
    chunks = tokens // 256
    result = pl.pallas_call(
        functools.partial(kernel, members, per_dev, stages),
        out_shape=jax.ShapeDtypeStruct((rows, members * out_cols), bf16),
        in_specs=[smem, smem, vmem, vmem, vmem, vmem, pl.BlockSpec(memory_space=pl.ANY)],
        out_specs=vmem,
        scratch_shapes=[
            head_buffer, head_buffer, head_buffer, head_buffer, head_buffer,
            pltpu.VMEM((cols, per_dev, tokens, width), bf16),
            pltpu.VMEM((cols, depth, out_cols), bf16),
            pltpu.VMEM((cols, depth, out_cols), bf16),
            pltpu.VMEM((tokens, out_cols), f32),
            pltpu.VMEM((tokens, out_cols), f32),
            pltpu.VMEM((tokens, out_cols), bf16),
            pltpu.VMEM((tokens, out_cols), bf16),
            pltpu.VMEM((tokens, out_cols), bf16),
            pltpu.VMEM((members, rows, out_cols), bf16),
            dma((per_dev, 3)), dma((per_dev, 3)), dma((per_dev, 3)),
            dma((2,)), dma,
            dma((per_dev, levels)), dma((per_dev, levels)), dma((cols, per_dev)),
            dma((chunks,)), dma((chunks,)),
            dma((members,)), dma((members,)),
        ],
        compiler_params=pltpu.CompilerParams(
            collective_id=0, has_side_effects=True, vmem_limit_bytes=48 * 1024 * 1024
        ),
        cost_estimate=pl.CostEstimate(
            flops=4 * tokens * tokens * depth + 2 * tokens * total * out_cols,
            bytes_accessed=2 * (3 * rows * total + total * out_cols + rows * members * out_cols),
            transcendentals=per_dev * tokens * tokens,
        ),
    )(head_class, kv_count, kv_blocks[0], queries[0], keys[0], values[0], weight)
    return result[None]


def solution(mesh):
    placed = (
        P("pipe", "seq", None),
        P("pipe", "seq", None),
        P("pipe", "seq", None),
        P("pipe", None, "seq"),
        P("pipe", None),
        P("pipe", None, None, None),
        P("pipe", None),
    )
    return jax.shard_map(
        functools.partial(shards, mesh.shape["pipe"]),
        mesh=mesh, in_specs=placed, out_specs=P("pipe", "seq", None), check_vma=False,
    )
```

time: 372 us -> 157 us (0.42); the launches traced: 367 us -> 156 us
  waiting for transfers between devices: 292 us -> 0 us
  Pallas kernels: 0 us -> 148 us
  starting transfers between devices: 24.5 us -> 0 us
  between operations: 19.6 us -> 0.05 us
  matrix products: 10.2 us -> 0 us
  local copies, waits for them, and re-layouts: 17 us -> 8.38 us
    reduce_scatter x1 -> x0, waiting for transfers between devices: 221 us -> none  [shards(): lax.psum_scatter(jnp.dot(joined, weight_mine, preferred_element_type=jnp....]
    pallas_call x0 -> x1, Pallas kernels: none -> 148 us  [shards(): pl.pallas_call(functools.partial(kernel, members, per_dev, stages), out_s...]
    all_to_all x4 -> x0, waiting for transfers between devices: 68.8 us -> none  [the longest x1 44.3 us: shards(): lax.all_to_all(weight_local, 'seq', split_axis=0, concat_axis=1, tiled=True)]
    all_to_all x4 -> x0, starting transfers between devices: 22.8 us -> none  [the longest x1 6.66 us: shards(): lax.all_to_all(query_rows, 'seq', split_axis=1, concat_axis=0, tiled=True)]
    dot_general x7 -> x0, matrix products: 10.2 us -> none  [the longest x1 7.3 us: shards(): jnp.dot(joined, weight_mine, preferred_element_type=jnp.float32)]
    all_to_all x4 -> x0, local copies, waits for them, and re-layouts: 5.34 us -> none  [the longest x1 2.47 us: shards(): lax.all_to_all(weight_local, 'seq', split_axis=0, concat_axis=1, tiled=True)]
    gather x6 -> x0, local copies, waits for them, and re-layouts: 3.89 us -> none  [the longest x3 1.94 us: advance(): value_blocks[chosen].reshape(nblock, 2 * BLOCK, head_width)]
    unnamed x17 -> x13, local copies, waits for them, and re-layouts: 5.19 us -> 8.38 us
  transfers between devices with their start and end apart: 6 -> 0, of which waited for: 6 -> 0; matrix products, arithmetic and copies ran while one was open for 5% -> 0% of each run, Pallas kernels for 0% -> 0%
where the time goes in v1:
time: 157 us; the launch traced here: 156 us
  Pallas kernels  148 us (94%)
  local copies, waits for them, and re-layouts  8.38 us (5%)
    pallas_call x1, Pallas kernels, shards(): pl.pallas_call(functools.partial(kernel, members, per_dev, stages), out_s...  148 us
    unnamed x13, local copies, waits for them, and re-layouts  8.38 us

profile of v1, /device:TPU:9, one launch (start us, length us, event | category | flops | bytes accessed | tf_op | source)
XLA Modules:
  0.0 156.4 jit_solution(18078735058180674022)
XLA Ops:
  0.0 0.0 copy-start.4
  0.0 0.0 copy-start.3
  0.0 1.1 copy.8
  1.1 3.3 %copy.9 = bf16[1,4096,320]{2,1,0:T(8,128)(2,1)S(1)} copy(bf16[1,4096,320]{1,2,0:T(8,128)(2,1)} %param.10) | data formatting | bytes 5242880 | tf_op args[3]
  4.4 0.0 copy-done.4
  4.4 0.0 copy-done.3
  4.5 0.0 copy-start
  4.5 1.0 copy-done
  5.5 0.0 copy-start.1
  5.5 1.0 copy-done.1
  6.5 0.0 copy-start.2
  6.5 1.0 copy-done.2
  7.6 148.0 %shard_map.73 = bf16[64,5120]{1,0:T(8,128)(2,1)S(1)} custom-call(s32[1,32]{1,0:T(1,128)S(1)} %copy-done.3, s32[1,32]{1,0:T(1,128)S(1)} %copy-done.4, s32[32,16,16]{2,1,0:T(8,128)S(1)} %bitcast.8, bf16[64,4096]{1,0:T(8,128)(2,1)S(1)} %bitcast.9, bf16[64,4096]{1,0:T(8,128)(2,1)S(1)} %bitcast.10, bf16[64,4096]{1,0:T(8,128)(2,1)S(1)} %bitcast.11, ...), custom_call_target="tpu_custom_call" | custom-call | flops 3758096384 | bytes 4849664 | tf_op jit(solution)/shard_map/pallas_call | solution.py:321
  155.5 0.8 copy.11
Async XLA Ops:
  0.0 4.4 %copy-start.4 = (s32[1,32]{1,0:T(1,128)S(1)}, s32[1,32]{1,0:T(1,128)}, u32[]{:S(2)}) copy-start(s32[1,32]{1,0:T(1,128)} %counts.1) | copy-start | bytes 388
  0.0 4.4 %copy-start.3 = (s32[1,32]{1,0:T(1,128)S(1)}, s32[1,32]{1,0:T(1,128)}, u32[]{:S(2)}) copy-start(s32[1,32]{1,0:T(1,128)} %classes.1) | copy-start | bytes 388
  4.5 1.0 copy-start
  5.5 1.0 copy-start.1
  6.5 1.0 copy-start.2

commit v2 on v1

v2 whole, which is shorter than its diff:
```python
import functools

import jax
import jax.numpy as jnp
from jax import lax
from jax.experimental import pallas as pl
from jax.experimental.pallas import tpu as pltpu
from jax.sharding import PartitionSpec as P

FRAMES = 4
BLOCK = 64
MASKED = 131072.0
LOG2E = 1.4426950408889634
TILE = 256
MESH = pl.DeviceIdType.MESH


def kernel(
    members, per_dev, stages,
    classes, counts, lists, queries, keys, values, weight,
    out,
    qbuf, kbuf, vbuf, ebuf, bbuf, abuf, wboth, cown, csend, crecv, osend, obuf,
    qkv_send, qkv_recv, qkv_local, w_sems, w_local, up_send, down_send, side_send, a_recv,
    c_send, c_recv, o_send, o_recv,
):
    stage = lax.axis_index("pipe")
    me = lax.axis_index("seq")
    half = lax.rem(me, 2)
    col = me // 2
    side = lax.rem(col, 2)
    level = col // 2
    levels = members // 4
    cols = members // 2
    partner = me + 1 - 2 * half
    across = me + 2 - 4 * side
    following = lax.rem(stage + 1, stages)
    preceding = lax.rem(stage + stages - 1, stages)
    rows, width = queries.shape[0], kbuf.shape[-1]
    tokens = rows * members
    depth = per_dev * width
    out_cols = weight.shape[0]
    tile = TILE
    chunks = tokens // tile
    group = tile // rows
    tensors = ((queries, qbuf), (keys, kbuf), (values, vbuf))

    def block_at(chunk, place):
        return place * chunks + lax.rem(chunk + place, chunks)

    barrier = pltpu.get_barrier_semaphore()

    def greet(r, carry):
        pl.semaphore_signal(
            barrier, inc=1, device_id={"seq": lax.rem(me + r, members)}, device_id_type=MESH
        )
        return carry

    def greet_preceding(r, carry):
        pl.semaphore_signal(barrier, inc=1, device_id=(preceding, r), device_id_type=MESH)
        return carry

    lax.fori_loop(1, members, greet, 0)
    lax.fori_loop(0, members, greet_preceding, 0)

    def head_columns(owner, slot):
        return pl.ds(pl.multiple_of((owner * per_dev + slot) * width, width), width)

    my_place = me // chunks
    my_chunk = lax.rem(lax.rem(me, chunks) + chunks * group - my_place, chunks)
    mine = pl.ds(pl.multiple_of((my_chunk * group + my_place) * rows, rows), rows)
    own_copies = []
    for slot in range(per_dev):
        for which, (source, landing) in enumerate(tensors):
            copy = pltpu.make_async_copy(
                source.at[:, head_columns(me, slot)],
                landing.at[slot, mine],
                qkv_local.at[slot, which],
            )
            copy.start()
            own_copies.append(copy)
    pl.semaphore_wait(barrier, 2 * members - 1)

    for slot in range(per_dev):

        def send(r, carry):
            peer = lax.rem(me + r, members)
            for which, (source, landing) in enumerate(tensors):
                pltpu.make_async_remote_copy(
                    src_ref=source.at[:, head_columns(peer, slot)],
                    dst_ref=landing.at[slot, mine],
                    send_sem=qkv_send.at[slot, which],
                    recv_sem=qkv_recv.at[slot, which],
                    device_id={"seq": peer},
                    device_id_type=MESH,
                ).start()
            return carry

        lax.fori_loop(1, members, send, 0)

    def weight_columns(column, which_half):
        return pl.ds(pl.multiple_of((2 * column + which_half) * depth, depth), depth)

    def own_weight(column, carry):
        pltpu.make_async_copy(
            weight.at[:, weight_columns(column, half)],
            wboth.at[pl.ds(0, out_cols), pl.ds(pl.multiple_of(column * depth, depth), depth)],
            w_local,
        ).start()
        return carry

    lax.fori_loop(0, cols, own_weight, 0)

    nblock = lists.shape[0]
    place = lax.broadcasted_iota(jnp.int32, (tokens, width), 0)
    lane = lax.broadcasted_iota(jnp.int32, (tokens, width), 1)
    token = block_at(place // tile, lax.rem(place, tile) // rows) * rows + lax.rem(place, rows)
    spatial = token // BLOCK
    temporal = lax.rem(token, tokens // FRAMES) // (BLOCK // FRAMES)
    every = lists[...].astype(jnp.float32)
    head_lane = lax.broadcasted_iota(jnp.int32, every.shape, 2)
    entry = lax.broadcasted_iota(jnp.int32, every.shape[:2] + (width,), 1)
    listed_lane = lax.broadcasted_iota(jnp.int32, entry.shape, 2).astype(jnp.float32)
    for slot in range(per_dev):
        head = me * per_dev + slot
        block_of = jnp.where(classes[0, head] == 1, temporal, spatial)
        member = jnp.where(block_of == lane, 1.0, 0.0).astype(jnp.bfloat16)
        ebuf[slot] = member
        entries = jnp.sum(jnp.where(head_lane == head, every, 0.0), axis=2, keepdims=True)
        usable = jnp.where(entry < counts[0, head], 0.0, -MASKED)
        offset = jnp.max(jnp.where(entries == listed_lane, usable, -MASKED), axis=1)
        offset = jnp.concatenate(
            [offset, jnp.zeros((width - nblock, width), jnp.float32)], axis=0
        ).astype(jnp.bfloat16)
        bbuf[slot] = lax.dot_general(
            member, offset, (((1,), (1,)), ((), ())), preferred_element_type=jnp.float32
        ).astype(jnp.bfloat16)
    for copy in own_copies:
        copy.wait()

    scale = LOG2E * width ** (-0.5)
    others = pl.ds(0, tokens - rows)

    def chunk_rows(chunk):
        return pl.ds(pl.multiple_of(chunk * tile, tile), tile)

    def piece_copy(source_level, slot, chunk, target, sems):
        column = 2 * source_level + side
        piece = abuf.at[column, slot, chunk_rows(chunk)]
        return pltpu.make_async_remote_copy(
            src_ref=piece,
            dst_ref=piece,
            send_sem=sems.at[slot, chunk, source_level],
            recv_sem=a_recv.at[column, slot, chunk],
            device_id={"seq": target},
            device_id_type=MESH,
        )

    def received(column, slot, chunk):
        piece = abuf.at[column, slot, chunk_rows(chunk)]
        pltpu.make_async_copy(piece, piece, a_recv.at[column, slot, chunk]).wait()

    def send_up(source_level, slot, chunk):
        @pl.when(level + 1 < levels)
        def _():
            piece_copy(source_level, slot, chunk, me + 4, up_send).start()

    def send_down(source_level, slot, chunk):
        @pl.when(level >= 1)
        def _():
            piece_copy(source_level, slot, chunk, me - 4, down_send).start()

    def send_side(source_level, slot, chunk):
        piece_copy(source_level, slot, chunk, across, side_send).start()

    def attend(slot):
        for which, (source, landing) in enumerate(tensors):
            span = landing.at[slot, others]
            pltpu.make_async_copy(span, span, qkv_recv.at[slot, which]).wait()

        def step(chunk, carry):
            here = chunk_rows(chunk)
            wide_query = jnp.concatenate([qbuf[slot, here], ebuf[slot, here]], axis=1)
            wide_key = jnp.concatenate([kbuf[slot], bbuf[slot]], axis=1)
            scores = lax.dot_general(
                wide_query, wide_key, (((1,), (1,)), ((), ())), preferred_element_type=jnp.float32
            )
            top = jnp.max(scores, axis=1, keepdims=True)
            probs = jnp.exp2((scores - top) * scale).astype(jnp.bfloat16)
            wide_value = jnp.concatenate(
                [vbuf[slot], jnp.ones((tokens, width), jnp.bfloat16)], axis=1
            )
            sums = jnp.dot(probs, wide_value, preferred_element_type=jnp.float32)
            abuf[col, slot, here] = (sums[:, :width] / sums[:, width:]).astype(jnp.bfloat16)
            send_up(level, slot, chunk)
            send_down(level, slot, chunk)
            send_side(level, slot, chunk)
            return carry

        lax.fori_loop(0, chunks, step, 0)

    def relay(slot, chunk):
        def hop(t, carry):
            below = level - 1 - t
            above = level + 1 + t

            @pl.when(below >= 0)
            def _():
                received(2 * below + side, slot, chunk)
                send_up(below, slot, chunk)
                send_side(below, slot, chunk)

            @pl.when(above < levels)
            def _():
                received(2 * above + side, slot, chunk)
                send_down(above, slot, chunk)
                send_side(above, slot, chunk)

            return carry

        lax.fori_loop(0, levels - 1, hop, 0)

    weight_span = wboth.at[pl.ds(out_cols, out_cols)]
    for slot in range(per_dev):
        attend(slot)
        if slot == 0:

            def swap_weight(column, carry):
                pltpu.make_async_remote_copy(
                    src_ref=weight.at[:, weight_columns(column, 1 - half)],
                    dst_ref=wboth.at[
                        pl.ds(out_cols, out_cols),
                        pl.ds(pl.multiple_of(column * depth, depth), depth),
                    ],
                    send_sem=w_sems.at[0],
                    recv_sem=w_sems.at[1],
                    device_id={"seq": partner},
                    device_id_type=MESH,
                ).start()
                return carry

            lax.fori_loop(0, cols, swap_weight, 0)
        if slot < per_dev - 1:

            def relay_step(chunk, carry):
                relay(slot, chunk)
                return carry

            lax.fori_loop(0, chunks, relay_step, 0)

    weight_own = wboth.at[pl.ds(0, out_cols)]
    pltpu.make_async_copy(weight_own, weight_own, w_local).wait()
    pltpu.make_async_copy(weight_span, weight_span, w_sems.at[1]).wait()

    def chunk_copy(chunk):
        here = chunk_rows(chunk)
        return pltpu.make_async_remote_copy(
            src_ref=csend.at[here],
            dst_ref=crecv.at[here],
            send_sem=c_send.at[chunk],
            recv_sem=c_recv.at[chunk],
            device_id={"seq": partner},
            device_id_type=MESH,
        )

    def row_copy(chunk, q):
        start = pl.multiple_of((chunk * group + q) * rows, rows)
        return pltpu.make_async_remote_copy(
            src_ref=osend.at[pl.ds(start, rows)],
            dst_ref=obuf.at[me],
            send_sem=o_send.at[chunk * group + q],
            recv_sem=o_recv.at[me],
            device_id=(following, block_at(chunk, q)),
            device_id_type=MESH,
        )

    def hand(chunk):
        here = chunk_rows(chunk)
        chunk_copy(chunk).wait_recv()
        osend[here] = (cown[here] + crecv[here].astype(jnp.float32)).astype(jnp.bfloat16)
        for q in range(group):
            row_copy(chunk, q).start()

    def finish(chunk, carry):
        here = chunk_rows(chunk)
        relay(per_dev - 1, chunk)

        def from_side(source_level, inner):
            for slot in range(per_dev):
                received(2 * source_level + 1 - side, slot, chunk)
            return inner

        lax.fori_loop(0, levels, from_side, 0)
        piece = jnp.concatenate(
            [abuf[column, slot, here] for column in range(cols) for slot in range(per_dev)], axis=1
        )
        shares = lax.dot_general(
            piece, wboth[...], (((1,), (1,)), ((), ())), preferred_element_type=jnp.float32
        )
        csend[here] = shares[:, out_cols:].astype(jnp.bfloat16)
        chunk_copy(chunk).start()
        cown[here] = shares[:, :out_cols]

        @pl.when(chunk >= 1)
        def _():
            hand(chunk - 1)

        return carry

    lax.fori_loop(0, chunks, finish, 0)
    hand(chunks - 1)

    for slot in range(per_dev):
        for which, (source, landing) in enumerate(tensors):
            span = landing.at[slot, others]
            pltpu.make_async_copy(span, span, qkv_send.at[slot, which]).wait()
    pltpu.make_async_copy(weight_span, weight_span, w_sems.at[0]).wait()

    def left(chunk, carry):
        for slot in range(per_dev):

            def from_level(source_level, inner):
                @pl.when((level + 1 < levels) & (source_level <= level))
                def _():
                    piece_copy(source_level, slot, chunk, across, up_send).wait_send()

                @pl.when((level >= 1) & (source_level >= level))
                def _():
                    piece_copy(source_level, slot, chunk, across, down_send).wait_send()

                piece_copy(source_level, slot, chunk, across, side_send).wait_send()
                return inner

            lax.fori_loop(0, levels, from_level, 0)
        chunk_copy(chunk).wait_send()
        for q in range(group):
            row_copy(chunk, q).wait_send()
        return carry

    lax.fori_loop(0, chunks, left, 0)

    def arrived(source, carry):
        pltpu.make_async_copy(obuf.at[source], obuf.at[source], o_recv.at[source]).wait()
        return carry

    lax.fori_loop(0, members, arrived, 0)
    pair = 2 * out_cols
    for i in range(members // 2):
        out[:, i * pair : (i + 1) * pair] = jnp.concatenate([obuf[2 * i], obuf[2 * i + 1]], axis=1)


def shards(stages, queries, keys, values, out_weight, head_class, kv_blocks, kv_count):
    members = lax.axis_size("seq")
    heads = head_class.shape[1]
    per_dev = heads // members
    rows, total = queries.shape[1:]
    width = total // heads
    tokens = rows * members
    out_cols = out_weight.shape[2]
    cols = members // 2
    depth = per_dev * width
    weight = out_weight[0].T
    bf16, f32 = jnp.bfloat16, jnp.float32
    dma = pltpu.SemaphoreType.DMA
    vmem = pl.BlockSpec(memory_space=pltpu.VMEM)
    smem = pl.BlockSpec(memory_space=pltpu.SMEM)
    hbm = pl.BlockSpec(memory_space=pl.ANY)
    head_buffer = pltpu.VMEM((per_dev, tokens, width), bf16)
    levels = members // 4
    chunks = tokens // TILE
    result = pl.pallas_call(
        functools.partial(kernel, members, per_dev, stages),
        out_shape=jax.ShapeDtypeStruct((rows, members * out_cols), bf16),
        in_specs=[smem, smem, vmem, hbm, hbm, hbm, hbm],
        out_specs=vmem,
        scratch_shapes=[
            head_buffer, head_buffer, head_buffer, head_buffer, head_buffer,
            pltpu.VMEM((cols, per_dev, tokens, width), bf16),
            pltpu.VMEM((2 * out_cols, cols * depth), bf16),
            pltpu.VMEM((tokens, out_cols), f32),
            pltpu.VMEM((tokens, out_cols), bf16),
            pltpu.VMEM((tokens, out_cols), bf16),
            pltpu.VMEM((tokens, out_cols), bf16),
            pltpu.VMEM((members, rows, out_cols), bf16),
            dma((per_dev, 3)), dma((per_dev, 3)), dma((per_dev, 3)),
            dma((2,)), dma,
            dma((per_dev, chunks, levels)), dma((per_dev, chunks, levels)),
            dma((per_dev, chunks, levels)), dma((cols, per_dev, chunks)),
            dma((chunks,)), dma((chunks,)),
            dma((members,)), dma((members,)),
        ],
        compiler_params=pltpu.CompilerParams(
            collective_id=0, has_side_effects=True, vmem_limit_bytes=60 * 1024 * 1024
        ),
        cost_estimate=pl.CostEstimate(
            flops=4 * tokens * tokens * depth + 2 * tokens * total * out_cols,
            bytes_accessed=2 * (3 * rows * total + total * out_cols + rows * members * out_cols),
            transcendentals=per_dev * tokens * tokens,
        ),
    )(head_class, kv_count, kv_blocks[0].transpose(1, 2, 0), queries[0], keys[0], values[0], weight)
    return result[None]


def solution(mesh):
    placed = (
        P("pipe", "seq", None),
        P("pipe", "seq", None),
        P("pipe", "seq", None),
        P("pipe", None, "seq"),
        P("pipe", None),
        P("pipe", None, None, None),
        P("pipe", None),
    )
    return jax.shard_map(
        functools.partial(shards, mesh.shape["pipe"]),
        mesh=mesh, in_specs=placed, out_specs=P("pipe", "seq", None), check_vma=False,
    )
```

time: 157 us -> 128 us (0.82)
  Pallas kernels: 148 us -> 126 us
  local copies, waits for them, and re-layouts: 8.38 us -> 1.97 us
    pallas_call x1, Pallas kernels: 148 us -> 126 us  [shards(): pl.pallas_call(functools.partial(kernel, members, per_dev, stages), out_s...]
    unnamed x13 -> x1, local copies, waits for them, and re-layouts: 8.38 us -> 1.97 us
where the time goes in v2:
time: 128 us
  Pallas kernels  126 us (98%)
  local copies, waits for them, and re-layouts  1.97 us (2%)
    pallas_call x1, Pallas kernels, shards(): pl.pallas_call(functools.partial(kernel, members, per_dev, stages), out_s...  126 us

profile of v2, /device:TPU:9, one launch (start us, length us, event | category | flops | bytes accessed | tf_op | source)
XLA Modules:
  0.0 127.8 jit_solution(4462184545557989957)
XLA Ops:
  0.0 125.9 %shard_map.73 = bf16[64,5120]{1,0:T(8,128)(2,1)} custom-call(s32[1,32]{1,0:T(1,128)} %classes.1, s32[1,32]{1,0:T(1,128)} %counts.1, s32[16,16,32]{2,1,0:T(8,128)} %bitcast.15, bf16[64,4096]{1,0:T(8,128)(2,1)} %bitcast.12, bf16[64,4096]{1,0:T(8,128)(2,1)} %bitcast.13, bf16[64,4096]{1,0:T(8,128)(2,1)} %bitcast.14, bf16[320,4096]{1,0:T(8,128)(2,1)} %bitcast.11), custom_call_target="tpu_custom_call" | custom-call | flops 3758096384 | bytes 4849664 | tf_op jit(solution)/shard_map/pallas_call | solution.py:370
  125.9 2.0 %copy.9 = bf16[1,64,5120]{2,1,0:T(8,128)(2,1)} copy(bf16[1,64,5120]{2,1,0:T(8,128)(2,1)} %bitcast.10) | data formatting | bytes 1310720
